TPU v7x, 32 devices: a whole 2x2x4 slice. The times are simulated.
32 devices in a mesh: group: 4 (over y, x), member: 8 (over z, core).
Axes of the slice: x: 2, y: 2, z: 4, core: 2. Of those that a mesh axis runs over, the one named last changes fastest.
Arguments:
- factor: float32 [4, 16, 768, 768], P('group', 'member'), as said below
- load: float32 [4, 16, 768], P('group', 'member'), may hold values from -6 to 6
- dof_map: int32 [4, 16, 768], P('group', 'member'), may hold values from 0 to 767, as said below
- dof_sign: int32 [4, 16, 768], P('group', 'member'), may hold values from -1 to 1, as said below
- live_count: int32 [4, 16], P('group', 'member'), may hold values from 384 to 768, as said below
- face_slot: int32 [4, 16, 4, 64], P('group', 'member'), may hold values from 0 to 767, as said below
- face_count: int32 [4, 16, 4], P('group', 'member'), may hold values from 0 to 64, as said below
- node_coord: int32 [4, 16, 3, 256], P('group', 'member'), may hold values from 0 to 15
- coarse_inverse: float32 [384, 384], P(('group', 'member')), as said below
Outputs:
- multipliers: float32 [4, 16, 768], P('group', 'member')
- projected: float32 [4, 16, 768], P('group', 'member')
Inputs may be any that keep to these rules, and one draw needn't show every extreme that they name: `dof_map`: each subdomain's row is a permutation of the unknowns. `dof_sign`: every entry is -1 or 1. `live_count`: in each cluster, both subdomains of one device have 768 live multipliers and both subdomains of the device whose member index differs by a quarter of 16 have 384. `face_slot`: the slots of one subdomain are distinct and below its live_count; slot k of a face pairs with slot k of the partner's face. `face_count`: A face and its partner's face have the same count; faces at the ends of a cluster's chain and at the first and last cluster have 0, all others 1 or more. `factor`: lower triangular with a positive diagonal. `coarse_inverse`: symmetric positive definite.
All inputs are finite; a program needn't handle non-finite values.
Results may differ from a plain program's by a relative error of at most 0.0003.
Values sent between devices are 32-bit elements; how exact they have to be, the bound alone decides.
A program may use at most 128 MiB of HBM per device.

v0:
```python
import math

import jax
import jax.numpy as jnp
from jax import lax
from jax.sharding import PartitionSpec as P

ITERS = 3


highest = lax.Precision.HIGHEST
half_span = 8.0


def padded(array, sides, width):
    for axis, dim in sides:
        size, length = (lax.axis_size(axis), array.shape[dim])
        up = [(i, (i + 1) % size) for i in range(size - 1)]
        down = [(j, i) for i, j in up]
        last = lax.slice_in_dim(array, length - width, length, axis=dim)
        leading = lax.slice_in_dim(array, 0, width, axis=dim)
        before = lax.ppermute(last, axis, up)
        after = lax.ppermute(leading, axis, down)
        array = jnp.concatenate([before, array, after], axis=dim)
    return array


def rigid_modes(node_coord):
    position = (node_coord.astype(jnp.float32) - half_span) / half_span
    spread = jnp.repeat(position, 3, axis=-1)
    component = jnp.arange(spread.shape[-1], dtype=jnp.int32) % 3
    first = (component == 0).astype(spread.dtype)
    second = (component == 1).astype(spread.dtype)
    third = (component == 2).astype(spread.dtype)
    coord_x = spread[..., 0, :]
    coord_y = spread[..., 1, :]
    coord_z = spread[..., 2, :]
    unit_row = jnp.ones_like(coord_x)
    return jnp.stack(
        [
            first * unit_row,
            second * unit_row,
            third * unit_row,
            third * coord_y - second * coord_z,
            first * coord_z - third * coord_x,
            second * coord_x - first * coord_y,
        ],
        axis=-2,
    )


def lower_solve(panel_matrix, right_side):
    return lax.linalg.triangular_solve(panel_matrix, right_side, left_side=True, lower=True)


def upper_solve(panel_matrix, right_side):
    return lax.linalg.triangular_solve(
        panel_matrix, right_side, left_side=True, lower=True, transpose_a=True
    )


def dual_of(panel_matrix, dof_codes, block_count, block_width):
    dof_count = panel_matrix.shape[0]
    slot_total = dof_codes.shape[0]
    levels = jnp.arange(dof_count, dtype=jnp.float32)[:, None]

    def solve_block(block_index, solved):
        columns = lax.dynamic_slice_in_dim(dof_codes, block_index * block_width, block_width)
        target = jnp.where(
            levels == jnp.abs(columns)[None, :] - 1.0, jnp.sign(columns)[None, :], 0.0
        )
        solved_piece = lower_solve(panel_matrix, target)
        return lax.dynamic_update_slice_in_dim(solved, solved_piece, block_index * block_width, 1)

    solved = lax.fori_loop(
        0, block_count, solve_block, jnp.zeros((dof_count, slot_total), jnp.float32)
    )

    def product_block(block_index, dual_sum):
        solved_piece = lax.dynamic_slice_in_dim(solved, block_index * block_width, block_width, 1)
        column = lax.dot_general(
            solved,
            solved_piece,
            (((0,), (0,)), ((), ())),
            precision=highest,
            preferred_element_type=jnp.float32,
        )
        return lax.dynamic_update_slice_in_dim(dual_sum, column, block_index * block_width, 1)

    return lax.fori_loop(
        0, block_count, product_block, jnp.zeros((slot_total, slot_total), jnp.float32)
    )


def shards(
    factor, load, dof_map, dof_sign, live_count, face_slot, face_count, node_coord, coarse_inverse
):
    own_panels = factor[0]
    own_loads = load[0]
    dof_count = own_loads.shape[1]
    subs_here = own_loads.shape[0]
    face_cap = face_slot.shape[3]
    block_width = math.gcd(dof_count, 128)
    positions = jnp.arange(dof_count, dtype=jnp.int32)
    live_mask = positions[None, :] < live_count[0][:, None]
    signed = jnp.where(live_mask, dof_sign[0], 0)
    dof_codes = ((dof_map[0] + 1) * signed).astype(jnp.float32)
    signed_float = signed.astype(jnp.float32)
    blocks_own = (live_count[0] + block_width - 1) // block_width
    first_dual = dual_of(own_panels[0], dof_codes[0], blocks_own[0], block_width)
    second_dual = dual_of(own_panels[1], dof_codes[1], blocks_own[1], block_width)
    dual_pair = jnp.stack([first_dual, second_dual])
    forward = jax.vmap(lambda panel_one, load_one: lower_solve(panel_one, load_one[:, None]))(
        own_panels, own_loads
    )
    displaced = jax.vmap(upper_solve)(own_panels, forward)[:, :, 0]
    gap_local = jnp.take_along_axis(displaced, dof_map[0], axis=1) * signed_float
    mode_table = rigid_modes(node_coord[0])
    rigid_rows = jnp.take_along_axis(
        mode_table, jnp.broadcast_to(dof_map[0][:, None, :], mode_table.shape), axis=2
    )
    rigid_rows = rigid_rows * signed_float[:, None, :]
    coarse_rhs = jnp.einsum("lai,li->la", mode_table, own_loads, precision=highest)
    slot_list = face_slot[0].reshape(subs_here, 4 * face_cap)
    slot_used = (
        jnp.arange(face_cap, dtype=jnp.int32)[None, None, :] < face_count[0][:, :, None]
    ).reshape(subs_here, 4 * face_cap)
    slot_table = (
        (slot_list[:, :, None] == positions[None, None, :]) & slot_used[:, :, None]
    ).astype(jnp.float32)
    shared = jnp.sum(slot_table, axis=1)
    weight = live_mask.astype(jnp.float32) * (1.0 - 0.5 * shared)

    def assemble(values):
        outgoing = jnp.einsum("lkj,lj->lk", slot_table, values, precision=highest)
        extended = padded(outgoing[None], (("group", 0), ("member", 1)), 1)
        incoming = jnp.stack(
            [
                jnp.concatenate(
                    [
                        extended[1, sub_index, face_cap : 2 * face_cap],
                        extended[1, sub_index + 2, 0:face_cap],
                        extended[0, sub_index + 1, 3 * face_cap : 4 * face_cap],
                        extended[2, sub_index + 1, 2 * face_cap : 3 * face_cap],
                    ]
                )
                for sub_index in range(subs_here)
            ]
        )
        return values + jnp.einsum("lk,lkj->lj", incoming, slot_table, precision=highest)

    def inner_part(left_field, right_field):
        return jnp.sum(weight * left_field * right_field)

    def global_sum(partial_value):
        return lax.psum(partial_value, ("group", "member"))

    def gather_coarse(local_coarse):
        return lax.all_gather(local_coarse.reshape(1, -1), ("group", "member"), axis=0, tiled=True)

    def coarse_of(values):
        return jnp.einsum("laj,lj->la", rigid_rows, values, precision=highest)

    def spread_modes(gathered):
        alpha = jnp.dot(coarse_inverse, gathered.reshape(-1), precision=highest).reshape(
            subs_here, -1
        )
        return assemble(jnp.einsum("laj,la->lj", rigid_rows, alpha, precision=highest))

    def apply_dual(values):
        return jnp.einsum("lij,lj->li", dual_pair, values, precision=highest)

    multipliers = spread_modes(gather_coarse(coarse_rhs))
    residual = assemble(gap_local - apply_dual(multipliers))
    coarse_res = gather_coarse(coarse_of(residual))
    projected = residual - spread_modes(coarse_res)
    direction = projected
    norm_now = global_sum(inner_part(projected, projected))
    for iteration in range(ITERS):
        image_vec = assemble(apply_dual(direction))
        curvature = global_sum(inner_part(direction, image_vec))
        step_size = norm_now / curvature
        multipliers = multipliers + step_size * direction
        residual = residual - step_size * image_vec
        coarse_res = gather_coarse(coarse_of(residual))
        projected = residual - spread_modes(coarse_res)
        norm_next = global_sum(inner_part(projected, projected))
        direction = projected + norm_next / norm_now * direction
        norm_now = norm_next
    return (multipliers[None], projected[None])


def solution(mesh):
    return jax.shard_map(
        shards,
        mesh=mesh,
        in_specs=(
            P("group", "member", None, None),
            P("group", "member", None),
            P("group", "member", None),
            P("group", "member", None),
            P("group", "member"),
            P("group", "member", None, None),
            P("group", "member", None),
            P("group", "member", None, None),
            P(("group", "member"), None),
        ),
        out_specs=(P("group", "member", None), P("group", "member", None)),
        check_vma=False,
    )
```

profile of v0, /device:TPU:0, one launch (start us, length us, event | category | flops | bytes accessed | tf_op | source)
XLA Modules:
  0.0 1881.5 jit_solution(3852254739839985720)
XLA Ops:
  4.6 71.1 %gather_fusion = f32[9216]{0:T(1024)S(1)} fusion(f32[2,6,768]{2,1,0:T(8,128)S(1)} %stack.120, s32[9216]{0:T(1024)S(1)} %reshape.406), kind=kCustom, calls=%fused_computation | custom fusion | bytes 184320 | tf_op jit(solution)/shard_map/jit(take_along_axis)/gather | solution.py:119
  76.0 43.0 %all-gather = f32[32,1,12]{2,1,0:T(1,128)S(1)} all-gather(f32[1,1,12]{2,1,0:T(1,128)S(1)} %reshape.418), channel_id=1, replica_groups=mesh['group'=4,'member'=8] {'group','member'}, dimensions={0}, use_global_device_ids=true | all-gather | bytes 1584 | tf_op jit(solution)/shard_map/all_gather | solution.py:159
  133.4 249.3 %while.57 = (s32[]{:T(128)}, f32[768,768]{1,0:T(8,128)}, s32[]{:T(128)}, f32[768]{0:T(1024)S(1)}, f32[768,768]{1,0:T(8,128)}, /*index=5*/s32[]{:T(128)}, s32[]{:T(128)}, s32[]{:T(128)}, s32[]{:T(128)}, s32[]{:T(128)}) while((s32[]{:T(128)}, f32[768,768]{1,0:T(8,128)}, s32[]{:T(128)}, f32[768]{0:T(1024)S(1)}, f32[768,768]{1,0:T(8,128)}, ...), condition=%wide.region_2.4_spmd.clone, body=%wide.region_1.3_spmd.clone.sunk | while | flops 530268544 | bytes 10424716 | solution.py:75
  152.3 59.8 %custom-call.41 = f32[6,128,128]{1,2,0:T(8,128)S(1)} custom-call(f32[6,128,128]{2,1,0:T(8,128)} %get-tuple-element.727), custom_call_target="InvertDiagBlocksLowerTriangular" | custom-call | tf_op jit(solution)/shard_map/while/body/triangular_solve/custom-call.1 | solution.py:53
  235.2 59.8 %custom-call.41 = f32[6,128,128]{1,2,0:T(8,128)S(1)} custom-call(f32[6,128,128]{2,1,0:T(8,128)} %get-tuple-element.727), custom_call_target="InvertDiagBlocksLowerTriangular" | custom-call | tf_op jit(solution)/shard_map/while/body/triangular_solve/custom-call.1 | solution.py:53
  318.1 59.8 %custom-call.41 = f32[6,128,128]{1,2,0:T(8,128)S(1)} custom-call(f32[6,128,128]{2,1,0:T(8,128)} %get-tuple-element.727), custom_call_target="InvertDiagBlocksLowerTriangular" | custom-call | tf_op jit(solution)/shard_map/while/body/triangular_solve/custom-call.1 | solution.py:53
  397.4 245.9 %while.59 = (s32[]{:T(128)}, f32[768,768]{1,0:T(8,128)}, s32[]{:T(128)}, f32[768]{0:T(1024)S(1)}, f32[768,768]{1,0:T(8,128)}, /*index=5*/s32[]{:T(128)}, s32[]{:T(128)}, s32[]{:T(128)}, s32[]{:T(128)}, s32[]{:T(128)}) while((s32[]{:T(128)}, f32[768,768]{1,0:T(8,128)}, s32[]{:T(128)}, f32[768]{0:T(1024)S(1)}, f32[768,768]{1,0:T(8,128)}, ...), condition=%wide.region_6.8_spmd.clone, body=%wide.region_5.7_spmd.clone.sunk | while | flops 530268544 | bytes 10424716 | solution.py:75
  415.3 59.8 %custom-call.44 = f32[6,128,128]{1,2,0:T(8,128)S(1)} custom-call(f32[6,128,128]{2,1,0:T(8,128)} %get-tuple-element.750), custom_call_target="InvertDiagBlocksLowerTriangular" | custom-call | tf_op jit(solution)/shard_map/while/body/triangular_solve/custom-call.1 | solution.py:53
  497.0 59.8 %custom-call.44 = f32[6,128,128]{1,2,0:T(8,128)S(1)} custom-call(f32[6,128,128]{2,1,0:T(8,128)} %get-tuple-element.750), custom_call_target="InvertDiagBlocksLowerTriangular" | custom-call | tf_op jit(solution)/shard_map/while/body/triangular_solve/custom-call.1 | solution.py:53
  578.7 59.8 %custom-call.44 = f32[6,128,128]{1,2,0:T(8,128)S(1)} custom-call(f32[6,128,128]{2,1,0:T(8,128)} %get-tuple-element.750), custom_call_target="InvertDiagBlocksLowerTriangular" | custom-call | tf_op jit(solution)/shard_map/while/body/triangular_solve/custom-call.1 | solution.py:53
  682.8 118.7 %custom-call.8 = f32[2,6,128,128]{2,3,1,0:T(8,128)S(1)} custom-call(f32[2,6,128,128]{3,2,1,0:T(8,128)} %bitcast.929), custom_call_target="InvertDiagBlocksLowerTriangular" | custom-call | tf_op jit(solution)/shard_map/vmap()/triangular_solve | solution.py:57
  832.9 260.2 %collective-permute-start.2 = (f32[3,1,256]{2,1,0:T(1,128)S(1)}, f32[3,1,256]{2,1,0:T(1,128)S(1)}, u32[]{:S(2)}, u32[]{:S(2)}) collective-permute-start(f32[3,1,256]{2,1,0:T(1,128)S(1)} %get-tuple-element.428), channel_id=1, source_target_pairs={{0,1},{1,2},{2,3},{3,4},{4,5},{5,6},{6,7},{8,9},{9,10},{10,11},{11... | collective-permute-start | bytes 9224 | tf_op jit(solution)/shard_map/ppermute | solution.py:22
  1094.6 83.3 %collective-permute-done.3 = f32[3,1,256]{2,1,0:T(1,128)S(1)} collective-permute-done((f32[3,1,256]{2,1,0:T(1,128)S(1)}, f32[3,1,256]{2,1,0:T(1,128)S(1)}, u32[]{:S(2)}, u32[]{:S(2)}) %collective-permute-start.3) | collective-permute-done | bytes 3104 | tf_op jit(solution)/shard_map/ppermute | solution.py:23
  1183.8 94.8 %collective-permute-start.4 = (f32[1,2,256]{2,1,0:T(2,128)S(1)}, f32[1,2,256]{2,1,0:T(2,128)S(1)}, u32[]{:S(2)}, u32[]{:S(2)}) collective-permute-start(f32[1,2,256]{2,1,0:T(2,128)S(1)} %bitcast.841), channel_id=1, source_target_pairs={{0,8},{8,16},{16,24},{1,9},{9,17},{17,25},{2,10},{10,18},{18,26},{... | collective-permute-start | bytes 6152 | tf_op jit(solution)/shard_map/ppermute | solution.py:22
  1280.0 91.8 %collective-permute-done.5 = f32[1,2,256]{2,1,0:T(2,128)S(1)} collective-permute-done((f32[1,2,256]{2,1,0:T(2,128)S(1)}, f32[1,2,256]{2,1,0:T(2,128)S(1)}, u32[]{:S(2)}, u32[]{:S(2)}) %collective-permute-start.5) | collective-permute-done | bytes 2080 | tf_op jit(solution)/shard_map/ppermute | solution.py:23
  1377.3 37.6 %all-gather.1 = f32[32,1,12]{2,1,0:T(1,128)S(1)} all-gather(f32[1,1,12]{2,1,0:T(1,128)S(1)} %reshape.420), channel_id=1, replica_groups=mesh['group'=4,'member'=8] {'group','member'}, dimensions={0}, use_global_device_ids=true | all-gather | bytes 1584 | tf_op jit(solution)/shard_map/all_gather | solution.py:159
  1455.0 40.2 %all-reduce = (f32[]{:T(128)}, f32[]{:T(128)}) all-reduce(f32[]{:T(128)} %get-tuple-element.296, f32[]{:T(128)} %get-tuple-element.295), channel_id=1, replica_groups=mesh['group'=4,'member'=8] {'group','member'}, use_global_device_ids=true, to_apply=%region_10.12 | all-reduce | flops 2 | bytes 16 | tf_op jit(solution)/shard_map/psum | solution.py:156
  1496.8 39.9 %all-gather.2 = f32[32,1,12]{2,1,0:T(1,128)S(1)} all-gather(f32[1,1,12]{2,1,0:T(1,128)S(1)} %reshape.422), channel_id=1, replica_groups=mesh['group'=4,'member'=8] {'group','member'}, dimensions={0}, use_global_device_ids=true | all-gather | bytes 1584 | tf_op jit(solution)/shard_map/all_gather | solution.py:159
  1552.6 41.4 %psum.44 = f32[]{:T(128)} all-reduce(f32[]{:T(128)} %fusion.181), channel_id=1, replica_groups=mesh['group'=4,'member'=8] {'group','member'}, use_global_device_ids=true, to_apply=%region_14.16 | all-reduce | flops 1 | bytes 8 | tf_op jit(solution)/shard_map/psum | solution.py:156
  1618.1 41.4 %psum.45 = f32[]{:T(128)} all-reduce(f32[]{:T(128)} %multiply_reduce_fusion.1), channel_id=1, replica_groups=mesh['group'=4,'member'=8] {'group','member'}, use_global_device_ids=true, to_apply=%region_16.18 | all-reduce | flops 1 | bytes 8 | tf_op jit(solution)/shard_map/psum | solution.py:156
  1661.2 40.3 %all-gather.3 = f32[32,1,12]{2,1,0:T(1,128)S(1)} all-gather(f32[1,1,12]{2,1,0:T(1,128)S(1)} %reshape.424), channel_id=1, replica_groups=mesh['group'=4,'member'=8] {'group','member'}, dimensions={0}, use_global_device_ids=true | all-gather | bytes 1584 | tf_op jit(solution)/shard_map/all_gather | solution.py:159
  1717.0 41.1 %psum.46 = f32[]{:T(128)} all-reduce(f32[]{:T(128)} %get-tuple-element.361), channel_id=1, replica_groups=mesh['group'=4,'member'=8] {'group','member'}, use_global_device_ids=true, to_apply=%region_18.20 | all-reduce | flops 1 | bytes 8 | tf_op jit(solution)/shard_map/psum | solution.py:156
  1782.3 41.4 %psum.47 = f32[]{:T(128)} all-reduce(f32[]{:T(128)} %multiply_reduce_fusion), channel_id=1, replica_groups=mesh['group'=4,'member'=8] {'group','member'}, use_global_device_ids=true, to_apply=%region_20.22 | all-reduce | flops 1 | bytes 8 | tf_op jit(solution)/shard_map/psum | solution.py:156
  1825.3 40.3 %all-gather.4 = f32[32,1,12]{2,1,0:T(1,128)S(1)} all-gather(f32[1,1,12]{2,1,0:T(1,128)S(1)} %reshape.426), channel_id=1, replica_groups=mesh['group'=4,'member'=8] {'group','member'}, dimensions={0}, use_global_device_ids=true | all-gather | bytes 1584 | tf_op jit(solution)/shard_map/all_gather | solution.py:159
  (606 shorter events, 516.4 us)
Async XLA Ops:
  122.3 710.6 %collective-permute-start = (f32[1,2,256]{2,1,0:T(2,128)S(1)}, f32[1,2,256]{2,1,0:T(2,128)S(1)}, u32[]{:S(2)}, u32[]{:S(2)}) collective-permute-start(f32[1,2,256]{2,1,0:T(2,128)S(1)} %bitcast.833), channel_id=1, source_target_pairs={{0,8},{8,16},{16,24},{1,9},{9,17},{17,25},{2,10},{10,18},{18,26},{... | collective-permute-start | bytes 6152 | tf_op jit(solution)/shard_map/ppermute | solution.py:22
  123.6 709.3 %collective-permute-start.1 = (f32[1,2,256]{2,1,0:T(2,128)S(1)}, f32[1,2,256]{2,1,0:T(2,128)S(1)}, u32[]{:S(2)}, u32[]{:S(2)}) collective-permute-start(f32[1,2,256]{2,1,0:T(2,128)S(1)} %bitcast.834), channel_id=1, source_target_pairs={{8,0},{16,8},{24,16},{9,1},{17,9},{25,17},{10,2},{18,10},{26,18},{... | collective-permute-start | bytes 6152 | tf_op jit(solution)/shard_map/ppermute | solution.py:23
  832.9 261.6 %collective-permute-start.2 = (f32[3,1,256]{2,1,0:T(1,128)S(1)}, f32[3,1,256]{2,1,0:T(1,128)S(1)}, u32[]{:S(2)}, u32[]{:S(2)}) collective-permute-start(f32[3,1,256]{2,1,0:T(1,128)S(1)} %get-tuple-element.428), channel_id=1, source_target_pairs={{0,1},{1,2},{2,3},{3,4},{4,5},{5,6},{6,7},{8,9},{9,10},{10,11},{11... | collective-permute-start | bytes 9224 | tf_op jit(solution)/shard_map/ppermute | solution.py:22
  1093.1 84.8 %collective-permute-start.3 = (f32[3,1,256]{2,1,0:T(1,128)S(1)}, f32[3,1,256]{2,1,0:T(1,128)S(1)}, u32[]{:S(2)}, u32[]{:S(2)}) collective-permute-start(f32[3,1,256]{2,1,0:T(1,128)S(1)} %get-tuple-element.429), channel_id=1, source_target_pairs={{1,0},{2,1},{3,2},{4,3},{5,4},{6,5},{7,6},{9,8},{10,9},{11,10},{12... | collective-permute-start | bytes 9224 | tf_op jit(solution)/shard_map/ppermute | solution.py:23
  1183.8 96.2 %collective-permute-start.4 = (f32[1,2,256]{2,1,0:T(2,128)S(1)}, f32[1,2,256]{2,1,0:T(2,128)S(1)}, u32[]{:S(2)}, u32[]{:S(2)}) collective-permute-start(f32[1,2,256]{2,1,0:T(2,128)S(1)} %bitcast.841), channel_id=1, source_target_pairs={{0,8},{8,16},{16,24},{1,9},{9,17},{17,25},{2,10},{10,18},{18,26},{... | collective-permute-start | bytes 6152 | tf_op jit(solution)/shard_map/ppermute | solution.py:22
  1278.7 93.2 %collective-permute-start.5 = (f32[1,2,256]{2,1,0:T(2,128)S(1)}, f32[1,2,256]{2,1,0:T(2,128)S(1)}, u32[]{:S(2)}, u32[]{:S(2)}) collective-permute-start(f32[1,2,256]{2,1,0:T(2,128)S(1)} %bitcast.842), channel_id=1, source_target_pairs={{8,0},{16,8},{24,16},{9,1},{17,9},{25,17},{10,2},{18,10},{26,18},{... | collective-permute-start | bytes 6152 | tf_op jit(solution)/shard_map/ppermute | solution.py:23
  1418.5 6.9 collective-permute-start.9
  1426.8 3.6 collective-permute-start.11
  1436.3 6.2 collective-permute-start.12
  1441.1 5.5 collective-permute-start.13
  1446.6 4.2 collective-permute-start.14
  1449.4 4.0 collective-permute-start.15
  1540.4 6.5 collective-permute-start.17
  1600.4 5.6 collective-permute-start.20
  1604.6 5.5 collective-permute-start.21
  1611.4 5.3 collective-permute-start.23
  1705.1 6.1 collective-permute-start.25
  1712.5 3.1 collective-permute-start.27
  1764.5 5.6 collective-permute-start.28
  1768.7 5.5 collective-permute-start.29
  1775.5 5.3 collective-permute-start.31
  1868.0 3.3 collective-permute-start.32
  1869.3 6.1 collective-permute-start.33
  1876.6 3.1 collective-permute-start.35
  (20 other events, 704.8 us)
where the time goes:
time: 1900 us; the launch traced here: 1880 us
  other arithmetic  509 us (27%)
  starting transfers between devices  410 us (22%)
  blocking collectives  407 us (21%)
  waiting for transfers between devices  225 us (12%)
  local copies, waits for them, and re-layouts  219 us (12%)
  matrix products  91.9 us (5%)
    ppermute x18, starting transfers between devices, padded(): before = lax.ppermute(last, axis, up)  387 us
    another operation x32, other arithmetic, lower_solve(): lax.linalg.triangular_solve(panel_matrix, right_side, left_side=True, low...  370 us
    ppermute x18, waiting for transfers between devices, padded(): after = lax.ppermute(leading, axis, down)  225 us
    psum x5, blocking collectives, global_sum(): return lax.psum(partial_value, ('group', 'member'))  206 us
    all_gather x5, blocking collectives, gather_coarse(): lax.all_gather(local_coarse.reshape(1, -1), ('group', 'member'), axis=0,...  201 us
    another operation x12, other arithmetic, upper_solve(): lax.linalg.triangular_solve(panel_matrix, right_side, left_side=True, low...  125 us
    another operation x116, local copies, waits for them, and re-layouts, lower_solve(): lax.linalg.triangular_solve(panel_matrix, right_side, left_side=True, low...  93.5 us
    gather x3, local copies, waits for them, and re-layouts, shards(): jnp.take_along_axis(mode_table, jnp.broadcast_to(dof_map[0][:, None, :],...  71.1 us
  transfers between devices with their start and end apart: 36, of which 17 were waited for; matrix products, arithmetic and copies ran while one was open for 37% of the time, Pallas kernels for 0%

commit v1 on v0

v1 whole, which is shorter than its diff:
```python
import functools

import jax
import jax.numpy as jnp
from jax import lax
from jax.experimental import pallas as pl
from jax.experimental.pallas import tpu as pltpu
from jax.sharding import PartitionSpec as P

ITERS = 3
BASE = 16
TILE = 128
HALF_SPAN = 8.0
LEFT, RIGHT, DOWN, UP = range(4)
F32 = jnp.float32
BF16 = jnp.bfloat16
NT = (((1,), (1,)), ((), ()))
NN = (((1,), (0,)), ((), ()))


def iota(shape, dim):
    return lax.broadcasted_iota(jnp.int32, shape, dim)


def dot(left, right, dims=NN):
    return lax.dot_general(left, right, dims, preferred_element_type=F32)


def parts_of(values, count):
    parts = []
    for _ in range(count):
        part = values.astype(BF16)
        parts.append(part)
        values = values - part.astype(F32)
    return parts


def mm(left, right):
    left_hi, left_lo = parts_of(left, 2)
    right_hi, right_lo = parts_of(right, 2)
    return dot(left_hi, right_hi) + (dot(left_hi, right_lo) + dot(left_lo, right_hi))


def row_times(rows, table, dims=NN):
    stacked = []
    for row in rows:
        for part in parts_of(row, 3):
            stacked.append(part.astype(F32))
    pad = -len(stacked) % 8
    stacked.append(jnp.zeros((pad, rows[0].shape[1]), F32))
    product = dot(jnp.concatenate(stacked, axis=0).astype(BF16), table, dims)
    return [
        product[3 * at : 3 * at + 1] + product[3 * at + 1 : 3 * at + 2] + product[3 * at + 2 : 3 * at + 3]
        for at in range(len(rows))
    ]


def invert(factor, linv, subs):
    size = factor.shape[1]
    blocks = size // TILE
    row = iota((TILE, TILE), 0)
    lane = iota((TILE, TILE), 1)
    shift = BASE.bit_length() - 1
    same = (row >> shift) == (lane >> shift)
    where_at = [(s, b) for s in range(subs) for b in range(blocks)]

    def diagonal(s, b):
        return factor[s, b * TILE : (b + 1) * TILE, b * TILE : (b + 1) * TILE]

    packed = []
    for s, b in where_at:
        kept = jnp.where(same, diagonal(s, b), 0.0)
        packed.append(jnp.sum(kept.reshape(TILE // BASE, BASE, TILE), axis=0))
    count = len(packed)
    packed = jnp.concatenate(packed, axis=0)
    wide = (TILE, BASE * TILE)
    source, target = iota(wide, 0), iota(wide, 1)
    spread = (((source & (BASE - 1)) == (target >> 7)) & ((source >> shift) == ((target & 127) >> shift)))
    spread = jnp.where(spread, 1.0, 0.0).astype(BF16)
    columns = sum(dot(part, spread) for part in parts_of(packed, 3))
    within = iota((count, BASE, TILE), 1)
    solved = jnp.where(within == (iota((count, BASE, TILE), 2) & (BASE - 1)), 1.0, 0.0)
    for m in range(BASE):
        column = columns[:, m * TILE : (m + 1) * TILE].reshape(count, BASE, TILE)
        pivot = solved[:, m : m + 1, :] / column[:, m : m + 1, :]
        solved = jnp.where(within > m, solved - column * pivot, jnp.where(within == m, pivot, solved))
    inverses = [
        jnp.where(same, jnp.concatenate([solved[at]] * (TILE // BASE), axis=0), 0.0) for at in range(count)
    ]
    width = BASE
    while width < TILE:
        level = width.bit_length() - 1
        below = (
            ((row >> (level + 1)) == (lane >> (level + 1)))
            & (((row >> level) & 1) == 1)
            & (((lane >> level) & 1) == 0)
        )
        middle = [
            mm(jnp.where(below, diagonal(s, b), 0.0), inverses[at]) for at, (s, b) in enumerate(where_at)
        ]
        inverses = [inverses[at] - mm(inverses[at], middle[at]) for at in range(count)]
        width *= 2
    for at, (s, b) in enumerate(where_at):
        rows = slice(b * TILE, (b + 1) * TILE)
        linv[s, rows, rows] = inverses[at]
        if b + 1 < blocks:
            linv[s, rows, (b + 1) * TILE :] = jnp.zeros((TILE, size - (b + 1) * TILE), F32)
    width = TILE
    while width < size:
        for start in range(0, size - width, 2 * width):
            middle_at, end = start + width, min(start + 2 * width, size)
            for s in range(subs):
                upper = linv[s, start:middle_at, start:middle_at]
                lower = linv[s, middle_at:end, middle_at:end]
                linv[s, middle_at:end, start:middle_at] = -mm(lower, mm(factor[s, middle_at:end, start:middle_at], upper))
        width *= 2


def setup_kernel(
    live, face_count, factor, load, dof_map, dof_sign, face_slot, coord,
    linv, pack, unpack, slots, mask, weight, modes, face_modes, rhs,
):
    subs, size = load.shape
    cap = face_slot.shape[2]
    nodes = coord.shape[2]
    for s in range(subs):
        sign_row = jnp.where(iota((1, size), 1) < live[s], dof_sign[s : s + 1, :].astype(F32), 0.0)
        slot_rows = jnp.where(iota((size, size), 0) == dof_map[s : s + 1, :], sign_row, 0.0).astype(BF16)
        slots[s] = slot_rows

        def table_of(order):
            face_row = jnp.concatenate([face_slot[s, f : f + 1, :] for f in order], axis=1)
            lane = iota((1, 4 * cap), 1)
            limit = jnp.zeros((1, 4 * cap), jnp.int32)
            for at, f in enumerate(order):
                limit = jnp.where(lane // cap == at, at * cap + face_count[s, f], limit)
            face_row = jnp.where(lane < limit, face_row, -1)
            hit = jnp.where(iota((size, 4 * cap), 0) == face_row, 1.0, 0.0).astype(BF16)
            return dot(slot_rows, hit).astype(BF16)

        outgoing = table_of((0, 1, 2, 3))
        pack[s] = outgoing
        unpack[s] = table_of((1, 0, 3, 2))
        live_row = jnp.abs(dot(jnp.ones((8, size), BF16), slot_rows, NT))[0:1]
        shared = dot(jnp.ones((8, 4 * cap), BF16), jnp.abs(outgoing), NT)[0:1]
        mask[s : s + 1, :] = live_row
        weight[s : s + 1, :] = live_row * (1.0 - 0.5 * shared)
        position = (coord[s].astype(F32) - HALF_SPAN) / HALF_SPAN
        stacked = jnp.concatenate(
            [position, iota((1, nodes), 1).astype(F32), jnp.zeros((4, nodes), F32)], axis=0
        ).astype(BF16)
        first_of = 3 * iota((nodes, size), 0)
        unknown = iota((nodes, size), 1)
        of_node = jnp.where((unknown >= first_of) & (unknown < first_of + 3), 1.0, 0.0).astype(BF16)
        spread = dot(stacked, of_node)
        x, y, z = spread[0:1], spread[1:2], spread[2:3]
        component = iota((1, size), 1).astype(F32) - 3.0 * spread[3:4]
        first = jnp.where(component == 0.0, 1.0, 0.0)
        second = jnp.where(component == 1.0, 1.0, 0.0)
        third = jnp.where(component == 2.0, 1.0, 0.0)
        table = jnp.concatenate(
            [
                first,
                second,
                third,
                third * y - second * z,
                first * z - third * x,
                second * x - first * y,
                jnp.zeros((2, size), F32),
            ],
            axis=0,
        )
        modes[s] = table * live_row
        face_modes[s] = dot(table.astype(BF16), outgoing)
        rhs[s] = jnp.broadcast_to(jnp.sum(table * load[s : s + 1, :], axis=1, keepdims=True), (8, TILE))
    invert(factor, linv, subs)


def pcg_kernel(
    groups, members,
    linv, pack, unpack, slots, mask, weight, load, modes, face_modes, rhs, coarse,
    out_multipliers, out_projected,
    inverse_rows, face_in, shape_rows, gather_in, gather_out, halo_in, halo_out,
    send_gather, recv_gather, send_halo, recv_halo, send_setup, recv_setup,
):
    subs, size = load.shape
    faces = pack.shape[2]
    cap = faces // 4
    total = groups * members
    span = 16 * groups
    width = coarse.shape[-1]
    message = gather_out.shape[-1]
    c, m = lax.axis_index("group"), lax.axis_index("member")
    me = c * members + m
    neighbours = (
        (m > 0, (c, lax.rem(m + members - 1, members))),
        (m < members - 1, (c, lax.rem(m + 1, members))),
        (c > 0, (lax.rem(c + groups - 1, groups), m)),
        (c < groups - 1, (lax.rem(c + 1, groups), m)),
    )
    opposite = (RIGHT, LEFT, UP, DOWN)

    def peer(step):
        other = lax.rem(me + step, total)
        return (other // members, lax.rem(other, members))

    inverse_rows[...] = jnp.zeros(inverse_rows.shape, F32)
    face_in[...] = jnp.zeros(face_in.shape, F32)
    halo_in[...] = jnp.zeros(halo_in.shape, F32)

    barrier = pltpu.get_barrier_semaphore()

    @pl.loop(1, total)
    def _(step):
        pl.semaphore_signal(barrier, inc=1, device_id=peer(step), device_id_type=pl.DeviceIdType.MESH)

    pl.semaphore_wait(barrier, total - 1)

    def remote(src, dst, send, recv, where):
        return pltpu.make_async_remote_copy(
            src_ref=src, dst_ref=dst, send_sem=send, recv_sem=recv,
            device_id=where, device_id_type=pl.DeviceIdType.MESH,
        )

    def sided(ref, way):
        if way == LEFT:
            return ref.at[0]
        return ref.at[1] if way == RIGHT else ref

    def halo_copy(turn, way):
        to = opposite[way]
        return remote(
            sided(halo_out.at[turn], way), sided(halo_in.at[turn, to], way),
            send_halo.at[turn, way], recv_halo.at[turn, to], neighbours[way][1],
        )

    def face_copy(way):
        to = opposite[way]
        return remote(
            sided(face_modes, way), sided(face_in.at[to], way),
            send_setup.at[0, way], recv_setup.at[0, to], neighbours[way][1],
        )

    def coarse_copy(way):
        to = opposite[way]
        return remote(
            sided(coarse, way),
            (inverse_rows.at[2, 1], inverse_rows.at[1, 0], inverse_rows.at[4], inverse_rows.at[3])[way],
            send_setup.at[1, way], recv_setup.at[1, to], neighbours[way][1],
        )

    def each_way(action):
        for way in range(4):
            @pl.when(neighbours[way][0])
            def _():
                action(way)

    def gather_start(turn, row):
        gather_out[turn] = row
        gather_in[turn, me] = row

        @pl.loop(1, total)
        def _(step):
            remote(
                gather_out.at[turn], gather_in.at[turn, me],
                send_gather.at[turn], recv_gather.at[turn], peer(step),
            ).start()

    def gather_view(turn):
        return gather_in.at[turn, pl.ds(0, total - 1)]

    def gather_wait(turn):
        view = gather_view(turn)
        pltpu.make_async_copy(view, view, recv_gather.at[turn]).wait()

    lane_row = iota((1, message), 1)

    def placing(s):
        at = iota((40, message), 0)
        lane = iota((40, message), 1)
        kind, a = at >> 3, at & 7
        own = 16 * c + 8 * s
        to_left = own - 8 if s == 1 else span + 16 * c + 8
        to_right = own + 8 if s == 0 else span + 16 * c
        base = jnp.where(kind == 0, own, jnp.where(kind == 1, to_left, jnp.where(
            kind == 2, to_right, jnp.where(kind == 3, own - 16, own + 16))))
        return jnp.where((lane == base + a) & (a < 6), 1.0, 0.0)

    places = [placing(s) for s in range(subs)]

    def coarse_sum(turn):
        summed = jnp.sum(gather_in[turn].reshape(groups, members, 1, message), axis=0).reshape(members, message)
        if span >= TILE:
            low, high = summed[:, :span], summed[:, span : 2 * span]
        else:
            lane = iota((members, message), 1)
            low = jnp.where(lane < span, summed, 0.0)
            high = jnp.where(lane < span, pltpu.roll(summed, message - span, 1), 0.0)
        second = ((iota((members, width), 1) >> 3) & 1) == 1
        none = jnp.zeros((1, width), F32)
        from_right = jnp.concatenate([high[1:], none], axis=0)
        from_left = jnp.concatenate([none, high[:-1]], axis=0)
        return low + jnp.where(second, from_right, from_left)

    def correction(coarse_values):
        fields = []
        for s in range(subs):
            spread = jnp.zeros((8, size), F32)
            for kind in range(5):
                product = jnp.zeros((8, width), F32)
                for at in range(members):
                    product = product + inverse_rows[kind, s, at] * coarse_values[at : at + 1, :]
                alpha = jnp.sum(product, axis=1, keepdims=True)
                spread = spread + shape_rows[s, 8 * kind : 8 * kind + 8, :] * alpha
            fields.append(jnp.sum(spread, axis=0, keepdims=True))
        return fields

    def apply_dual(fields):
        images = []
        for s in range(subs):
            sums = [jnp.zeros((8, TILE), F32) for _ in range(size // TILE)]
            for b in range(size // TILE):
                reach = (b + 1) * TILE
                panel = linv[s, b * TILE : reach, :reach]
                column = jnp.sum(panel * fields[s][:, :reach], axis=1, keepdims=True)
                for at in range(b + 1):
                    piece = panel[:, at * TILE : (at + 1) * TILE] * column
                    sums[at] = sums[at] + jnp.sum(piece.reshape(TILE // 8, 8, TILE), axis=0)
            image = jnp.concatenate([jnp.sum(part, axis=0, keepdims=True) for part in sums], axis=1)
            images.append(image * mask[s : s + 1, :])
        return images

    face_lane = iota((1, faces), 1)

    def from_faces(right, left, up, down):
        return jnp.where(
            face_lane < cap, right,
            jnp.where(face_lane < 2 * cap, left, jnp.where(face_lane < 3 * cap, up, down)),
        )

    def project(turn, fields, scalars):
        outgoing = [row_times([fields[s]], pack[s])[0] for s in range(subs)]
        for s in range(subs):
            halo_out[turn - 1, s] = outgoing[s]
        each_way(lambda way: halo_copy(turn - 1, way).start())
        row = jnp.zeros((1, message), F32)
        for s in range(subs):
            column = jnp.sum(shape_rows[s] * fields[s], axis=1, keepdims=True)
            row = row + jnp.sum(places[s] * column, axis=0, keepdims=True)
        spare = (6, 7, 14)
        for at, value in enumerate(scalars):
            row = row + jnp.where(lane_row == 16 * c + spare[at], value, 0.0)
        gather_start(turn, row)
        each_way(lambda way: halo_copy(turn - 1, opposite[way]).wait_recv())
        arrived = halo_in.at[turn - 1]
        rights = (outgoing[1], arrived[RIGHT, 0])
        lefts = (arrived[LEFT, 1], outgoing[0])
        assembled = []
        for s in range(subs):
            incoming = from_faces(rights[s], lefts[s], arrived[UP, s], arrived[DOWN, s])
            assembled.append(fields[s] + row_times([incoming], unpack[s], NT)[0])
        gather_wait(turn)
        values = coarse_sum(turn)
        fixes = correction(values)
        spare_lane = iota(values.shape, 1) & 15
        sums = []
        for at in range(len(scalars)):
            kept = jnp.where(spare_lane == spare[at], values, 0.0)
            sums.append(jnp.sum(jnp.sum(kept, axis=1, keepdims=True), axis=0, keepdims=True))
        return [assembled[s] - fixes[s] for s in range(subs)], sums

    each_way(lambda way: face_copy(way).start())
    each_way(lambda way: coarse_copy(way).start())
    row = jnp.zeros((1, message), F32)
    for s in range(subs):
        column = jnp.concatenate([rhs[s][:, 0:1], jnp.zeros((32, 1), F32)], axis=0)
        row = row + jnp.sum(places[s] * column, axis=0, keepdims=True)
    gather_start(0, row)
    for s in range(subs):
        inverse_rows[0, s] = coarse[s]
    inverse_rows[2, 0] = coarse[1]
    inverse_rows[1, 1] = coarse[0]
    each_way(lambda way: face_copy(opposite[way]).wait_recv())
    each_way(lambda way: coarse_copy(opposite[way]).wait_recv())
    rights = (face_modes[1], face_in[RIGHT, 0])
    lefts = (face_in[LEFT, 1], face_modes[0])
    block = iota((8, faces), 1) // cap
    for s in range(subs):
        sources = (lefts[s], rights[s], face_in[DOWN, s], face_in[UP, s])
        spread = jnp.concatenate(
            [jnp.where(block == (1, 0, 3, 2)[f], sources[f], 0.0) for f in range(4)], axis=0
        ).astype(BF16)
        shape_rows[s, 0:8, :] = modes[s]
        shape_rows[s, 8:40, :] = dot(spread, unpack[s], NT)
    gather_wait(0)
    multipliers = correction(coarse_sum(0))
    start = apply_dual([load[s : s + 1, :] - multipliers[s] for s in range(subs)])
    projected, _ = project(1, start, [])
    for turn in range(ITERS):
        image = apply_dual(projected)
        norm = sum(
            jnp.sum(weight[s : s + 1, :] * projected[s] * projected[s], axis=1, keepdims=True) for s in range(subs)
        )
        energy = sum(jnp.sum(projected[s] * image[s], axis=1, keepdims=True) for s in range(subs))
        partials = [norm, energy]
        if turn:
            partials.append(
                sum(jnp.sum(projected[s] * direction_image[s], axis=1, keepdims=True) for s in range(subs))
            )
        change, sums = project(2 + turn, image, partials)
        if turn:
            ratio = sums[0] / norm_now
            curvature = sums[1] + 2.0 * ratio * sums[2] + ratio * ratio * curvature
            direction = [projected[s] + ratio * direction[s] for s in range(subs)]
            direction_image = [image[s] + ratio * direction_image[s] for s in range(subs)]
            direction_change = [change[s] + ratio * direction_change[s] for s in range(subs)]
        else:
            curvature = sums[1]
            direction, direction_image, direction_change = projected, image, change
        norm_now = sums[0]
        step = norm_now / curvature
        multipliers = [multipliers[s] + step * direction[s] for s in range(subs)]
        projected = [projected[s] - step * direction_change[s] for s in range(subs)]
    for s in range(subs):
        ordered = row_times([multipliers[s], projected[s]], slots[s])
        out_multipliers[s : s + 1, :] = ordered[0]
        out_projected[s : s + 1, :] = ordered[1]

    each_way(lambda way: face_copy(way).wait_send())
    each_way(lambda way: coarse_copy(way).wait_send())
    for turn in range(ITERS + 1):
        each_way(lambda way: halo_copy(turn, way).wait_send())
    for turn in range(ITERS + 2):
        view = gather_view(turn)
        pltpu.make_async_copy(view, view, send_gather.at[turn]).wait()


def shards(
    groups, members,
    factor, load, dof_map, dof_sign, live_count, face_slot, face_count, node_coord, coarse_inverse,
):
    subs, size = load.shape[1:]
    faces = 4 * face_slot.shape[3]
    span = 16 * groups
    width = -(-span // TILE) * TILE
    message = -(-2 * span // TILE) * TILE
    vmem = pl.BlockSpec(memory_space=pltpu.VMEM)
    smem = pl.BlockSpec(memory_space=pltpu.SMEM)
    shape = jax.ShapeDtypeStruct
    prepared = pl.pallas_call(
        setup_kernel,
        name="setup",
        out_shape=(
            shape((subs, size, size), F32),
            shape((subs, size, faces), BF16),
            shape((subs, size, faces), BF16),
            shape((subs, size, size), BF16),
            shape((subs, size), F32),
            shape((subs, size), F32),
            shape((subs, 8, size), F32),
            shape((subs, 8, faces), F32),
            shape((subs, 8, TILE), F32),
        ),
        in_specs=[smem, smem] + [vmem] * 6,
        out_specs=[vmem] * 9,
        compiler_params=pltpu.CompilerParams(vmem_limit_bytes=48 * 2**20),
    )(
        live_count[0], face_count[0], factor[0], load[0], dof_map[0], dof_sign[0], face_slot[0], node_coord[0]
    )
    rows = coarse_inverse.reshape(subs, 6, groups, members, subs, 6)
    rows = jnp.pad(rows, ((0, 0), (0, 2), (0, 0), (0, 0), (0, 0), (0, 2)))
    rows = rows.transpose(0, 3, 1, 2, 4, 5).reshape(subs, members, 8, span)
    rows = jnp.pad(rows, ((0, 0), (0, 0), (0, 0), (0, width - span)))
    linv, pack, unpack, slots, mask, weight, modes, face_modes, rhs = prepared
    turns = ITERS + 2
    multipliers, projected = pl.pallas_call(
        functools.partial(pcg_kernel, groups, members),
        name="pcg",
        out_shape=(shape((subs, size), F32), shape((subs, size), F32)),
        in_specs=[vmem] * 11,
        out_specs=[vmem] * 2,
        scratch_shapes=[
            pltpu.VMEM((5, subs, members, 8, width), F32),
            pltpu.VMEM((4, subs, 8, faces), F32),
            pltpu.VMEM((subs, 40, size), F32),
            pltpu.VMEM((turns, groups * members, 1, message), F32),
            pltpu.VMEM((turns, 1, message), F32),
            pltpu.VMEM((turns - 1, 4, subs, 1, faces), F32),
            pltpu.VMEM((turns - 1, subs, 1, faces), F32),
            pltpu.SemaphoreType.DMA((turns,)),
            pltpu.SemaphoreType.DMA((turns,)),
            pltpu.SemaphoreType.DMA((turns - 1, 4)),
            pltpu.SemaphoreType.DMA((turns - 1, 4)),
            pltpu.SemaphoreType.DMA((2, 4)),
            pltpu.SemaphoreType.DMA((2, 4)),
        ],
        compiler_params=pltpu.CompilerParams(
            collective_id=0, has_side_effects=True, vmem_limit_bytes=48 * 2**20
        ),
    )(linv, pack, unpack, slots, mask, weight, load[0], modes, face_modes, rhs, rows)
    return multipliers[None], projected[None]


def solution(mesh):
    return jax.shard_map(
        functools.partial(shards, mesh.shape["group"], mesh.shape["member"]),
        mesh=mesh,
        in_specs=(
            P("group", "member", None, None),
            P("group", "member", None),
            P("group", "member", None),
            P("group", "member", None),
            P("group", "member"),
            P("group", "member", None, None),
            P("group", "member", None),
            P("group", "member", None, None),
            P(("group", "member"), None),
        ),
        out_specs=(P("group", "member", None), P("group", "member", None)),
        check_vma=False,
    )
```

time: 1900 us -> 61.3 us (0.03)
  other arithmetic: 509 us -> 0 us
  starting transfers between devices: 410 us -> 0 us
  blocking collectives: 407 us -> 0 us
  waiting for transfers between devices: 225 us -> 0 us
  local copies, waits for them, and re-layouts: 219 us -> 8.42 us
  matrix products: 91.9 us -> 0 us
  Pallas kernels: 0 us -> 51.8 us
    another operation x53 -> x0, other arithmetic: 494 us -> none  [the longest x32 370 us: lower_solve(): lax.linalg.triangular_solve(panel_matrix, right_side, left_side=True, low...]
    ppermute x36 -> x0, starting transfers between devices: 410 us -> none  [the longest x18 387 us: padded(): before = lax.ppermute(last, axis, up)]
    ppermute x36 -> x0, waiting for transfers between devices: 225 us -> none  [the longest x18 225 us: padded(): after = lax.ppermute(leading, axis, down)]
    psum x5 -> x0, blocking collectives: 206 us -> none  [global_sum(): return lax.psum(partial_value, ('group', 'member'))]
    all_gather x5 -> x0, blocking collectives: 201 us -> none  [gather_coarse(): lax.all_gather(local_coarse.reshape(1, -1), ('group', 'member'), axis=0,...]
    another operation x145 -> x0, local copies, waits for them, and re-layouts: 119 us -> none  [the longest x116 93.5 us: lower_solve(): lax.linalg.triangular_solve(panel_matrix, right_side, left_side=True, low...]
    gather x6 -> x0, local copies, waits for them, and re-layouts: 84.6 us -> none  [the longest x3 71.1 us: shards(): jnp.take_along_axis(mode_table, jnp.broadcast_to(dof_map[0][:, None, :],...]
    dot_general x43 -> x0, matrix products: 54.2 us -> none  [the longest x6 19.6 us: product_block(): lax.dot_general(solved, solved_piece, (((0,), (0,)), ((), ())), precision...]
  transfers between devices with their start and end apart: 36 -> 0, of which waited for: 17 -> 0; matrix products, arithmetic and copies ran while one was open for 37% -> 0% of each run, Pallas kernels for 0% -> 0%
where the time goes in v1:
time: 61.3 us; the launch traced here: 60.9 us
  Pallas kernels  51.8 us (85%)
  local copies, waits for them, and re-layouts  8.42 us (14%)
  between operations  0.68 us (1%)
    pallas_call x1, Pallas kernels, shards(): pl.pallas_call(functools.partial(pcg_kernel, groups, members), name='pcg'...  39 us
    pallas_call x1, Pallas kernels, shards(): pl.pallas_call(setup_kernel, name='setup', out_shape=(shape((subs, size,...  12.8 us
    unnamed x15, local copies, waits for them, and re-layouts  5.97 us
    reshape x1, local copies, waits for them, and re-layouts, shards(): rows = coarse_inverse.reshape(subs, 6, groups, members, subs, 6)  1.32 us

profile of v1, /device:TPU:0, one launch (start us, length us, event | category | flops | bytes accessed | tf_op | source)
XLA Modules:
  0.0 60.9 jit_solution(3726833529006690181)
XLA Ops:
  0.6 0.7 %copy.16 = s32[1,2,3,256]{3,2,1,0:T(4,128)S(1)} copy(s32[1,2,3,256]{3,1,2,0:T(2,128)} %param.16) | data formatting | bytes 12288 | tf_op args[7]
  1.3 1.3 %reshape.10 = f32[2,6,4,8,2,6]{5,4,3,2,1,0:T(2,128)S(1)} reshape(f32[12,384]{1,0:T(8,128)} %param.17) | data formatting | bytes 36864 | tf_op jit(solution)/shard_map/reshape | solution.py:470
  2.7 0.2 pad_bitcast_fusion
  2.9 0.2 copy.14
  3.1 0.7 %reshape.11 = f32[2,8,8,64]{3,2,1,0:T(8,128)S(1)} reshape(f32[2,8,8,4,2,8]{5,4,3,2,1,0:T(2,128)S(1)} %copy.14) | data formatting | bytes 65536 | tf_op jit(solution)/shard_map/reshape | solution.py:472
  3.8 0.0 copy-start
  3.8 0.7 %copy-done = f32[1,2,768]{2,1,0:T(2,128)S(1)} copy-done((f32[1,2,768]{2,1,0:T(2,128)S(1)}, f32[1,2,768]{2,1,0:T(2,128)}, u32[]{:S(2)}) %copy-start) | copy-done | bytes 6168
  4.5 0.0 copy-start.1
  4.5 0.7 %copy-done.1 = s32[1,2,768]{2,1,0:T(2,128)S(1)} copy-done((s32[1,2,768]{2,1,0:T(2,128)S(1)}, s32[1,2,768]{2,1,0:T(2,128)}, u32[]{:S(2)}) %copy-start.1) | copy-done | bytes 6168
  5.2 0.0 copy-start.2
  5.2 0.7 %copy-done.2 = s32[1,2,768]{2,1,0:T(2,128)S(1)} copy-done((s32[1,2,768]{2,1,0:T(2,128)S(1)}, s32[1,2,768]{2,1,0:T(2,128)}, u32[]{:S(2)}) %copy-start.2) | copy-done | bytes 6168
  5.9 0.0 copy-start.3
  5.9 0.7 %copy-done.3 = s32[1,2,4,64]{3,2,1,0:T(4,128)S(1)} copy-done((s32[1,2,4,64]{3,2,1,0:T(4,128)S(1)}, s32[1,2,4,64]{3,2,1,0:T(4,128)}, u32[]{:S(2)}) %copy-start.3) | copy-done | bytes 2072
  6.6 0.0 copy-start.4
  6.6 0.7 %copy-done.4 = s32[1,2,4]{2,1,0:T(2,128)S(1)} copy-done((s32[1,2,4]{2,1,0:T(2,128)S(1)}, s32[1,2,4]{2,1,0:T(2,128)}, u32[]{:S(2)}) %copy-start.4) | copy-done | bytes 56
  7.3 0.0 copy-start.5
  7.3 0.7 %copy-done.5 = s32[1,2]{1,0:T(1,128)S(1)} copy-done((s32[1,2]{1,0:T(1,128)S(1)}, s32[1,2]{1,0:T(1,128)}, u32[]{:S(2)}) %copy-start.5) | copy-done | bytes 32
  7.9 12.8 %setup.1 = (f32[2,768,768]{2,1,0:T(8,128)}, bf16[2,768,256]{2,1,0:T(8,128)(2,1)S(1)}, bf16[2,768,256]{2,1,0:T(8,128)(2,1)S(1)}, bf16[2,768,768]{2,1,0:T(8,128)(2...) custom-call(s32[2]{0:T(128)S(1)} %bitcast.23, ...), custom_call_target="tpu_custom_call" | custom-call | tf_op jit(solution)/shard_map/setup/pallas_call | solution.py:450
  20.7 39.0 %pcg.1 = (f32[2,768]{1,0:T(2,128)S(1)}, f32[2,768]{1,0:T(2,128)S(1)}) custom-call(f32[2,768,768]{2,1,0:T(8,128)} %get-tuple-element.13.linv, bf16[2,768,256]{2,1,0:T(8,128)(2,1)S(1)} %get-tuple-element.14.pack, bf16[2,768,256]{2,1,0:T(8,128)(2,1)S(1)} %get-tuple-element.15.unpack, bf16[2,768,768]{2,1,0:T(8,128)(2,1)S(1)} %get-tuple-element.16.slots, ...), custom_call_target="tpu_custom_call" | custom-call | tf_op jit(solution)/shard_map/pcg/pallas_call | solution.py:476
  59.7 0.6 copy.19
  60.3 0.6 copy.20
  (1 shorter events, 0.0 us)
Async XLA Ops:
  3.8 0.7 %copy-start = (f32[1,2,768]{2,1,0:T(2,128)S(1)}, f32[1,2,768]{2,1,0:T(2,128)}, u32[]{:S(2)}) copy-start(f32[1,2,768]{2,1,0:T(2,128)} %param.10) | copy-start | bytes 18436
  4.5 0.7 %copy-start.1 = (s32[1,2,768]{2,1,0:T(2,128)S(1)}, s32[1,2,768]{2,1,0:T(2,128)}, u32[]{:S(2)}) copy-start(s32[1,2,768]{2,1,0:T(2,128)} %param.11) | copy-start | bytes 18436
  5.2 0.7 %copy-start.2 = (s32[1,2,768]{2,1,0:T(2,128)S(1)}, s32[1,2,768]{2,1,0:T(2,128)}, u32[]{:S(2)}) copy-start(s32[1,2,768]{2,1,0:T(2,128)} %param.12) | copy-start | bytes 18436
  5.9 0.7 %copy-start.3 = (s32[1,2,4,64]{3,2,1,0:T(4,128)S(1)}, s32[1,2,4,64]{3,2,1,0:T(4,128)}, u32[]{:S(2)}) copy-start(s32[1,2,4,64]{3,2,1,0:T(4,128)} %param.14) | copy-start | bytes 6148
  6.6 0.7 %copy-start.4 = (s32[1,2,4]{2,1,0:T(2,128)S(1)}, s32[1,2,4]{2,1,0:T(2,128)}, u32[]{:S(2)}) copy-start(s32[1,2,4]{2,1,0:T(2,128)} %param.15) | copy-start | bytes 100
  7.3 0.7 %copy-start.5 = (s32[1,2]{1,0:T(1,128)S(1)}, s32[1,2]{1,0:T(1,128)}, u32[]{:S(2)}) copy-start(s32[1,2]{1,0:T(1,128)} %param.13) | copy-start | bytes 28

commit v2 on v1

--- a/solution.py
+++ b/solution.py
@@ -11,6 +11,7 @@
 BASE = 16
 TILE = 128
 HALF_SPAN = 8.0
+VMEM_LIMIT = 62 * 2**20
 LEFT, RIGHT, DOWN, UP = range(4)
 F32 = jnp.float32
 BF16 = jnp.bfloat16
@@ -116,15 +117,15 @@
         width *= 2
 
 
-def setup_kernel(
-    live, face_count, factor, load, dof_map, dof_sign, face_slot, coord,
-    linv, pack, unpack, slots, mask, weight, modes, face_modes, rhs,
+def tables(
+    live, face_count, load, dof_map, dof_sign, face_slot, coord,
+    pack, unpack, slots, mask, weight, modes, face_modes, rhs,
 ):
     subs, size = load.shape
     cap = face_slot.shape[2]
     nodes = coord.shape[2]
     for s in range(subs):
-        sign_row = jnp.where(iota((1, size), 1) < live[s], dof_sign[s : s + 1, :].astype(F32), 0.0)
+        sign_row = jnp.where(iota((1, size), 1) < live[0:1, s : s + 1], dof_sign[s : s + 1, :].astype(F32), 0.0)
         slot_rows = jnp.where(iota((size, size), 0) == dof_map[s : s + 1, :], sign_row, 0.0).astype(BF16)
         slots[s] = slot_rows
 
@@ -133,7 +134,7 @@
             lane = iota((1, 4 * cap), 1)
             limit = jnp.zeros((1, 4 * cap), jnp.int32)
             for at, f in enumerate(order):
-                limit = jnp.where(lane // cap == at, at * cap + face_count[s, f], limit)
+                limit = jnp.where(lane // cap == at, at * cap + face_count[s : s + 1, f : f + 1], limit)
             face_row = jnp.where(lane < limit, face_row, -1)
             hit = jnp.where(iota((size, 4 * cap), 0) == face_row, 1.0, 0.0).astype(BF16)
             return dot(slot_rows, hit).astype(BF16)
@@ -145,7 +146,8 @@
         shared = dot(jnp.ones((8, 4 * cap), BF16), jnp.abs(outgoing), NT)[0:1]
         mask[s : s + 1, :] = live_row
         weight[s : s + 1, :] = live_row * (1.0 - 0.5 * shared)
-        position = (coord[s].astype(F32) - HALF_SPAN) / HALF_SPAN
+        position = jnp.concatenate([coord[axis, s : s + 1, :] for axis in range(3)], axis=0)
+        position = (position.astype(F32) - HALF_SPAN) / HALF_SPAN
         stacked = jnp.concatenate(
             [position, iota((1, nodes), 1).astype(F32), jnp.zeros((4, nodes), F32)], axis=0
         ).astype(BF16)
@@ -173,16 +175,48 @@
         modes[s] = table * live_row
         face_modes[s] = dot(table.astype(BF16), outgoing)
         rhs[s] = jnp.broadcast_to(jnp.sum(table * load[s : s + 1, :], axis=1, keepdims=True), (8, TILE))
-    invert(factor, linv, subs)
+
+
+def coarse_layout(raw, coarse, groups, members):
+    width = coarse.shape[-1]
+    none = jnp.zeros((2, raw.shape[1]), F32)
+    rows = jnp.concatenate([raw[0:6, :], none, raw[6:12, :], none], axis=0)
+    stacked = jnp.concatenate([part.astype(F32) for part in parts_of(rows, 3)], axis=0).astype(BF16)
+
+    def one(at, carry):
+        lane = iota((1, width), 1)
+        column = 12 * ((lane >> 4) * members + at) + 6 * ((lane >> 3) & 1) + (lane & 7)
+        column = jnp.where(((lane & 7) < 6) & (lane < 16 * groups), column, -1)
+        pick = jnp.where(iota((raw.shape[1], width), 0) == column, 1.0, 0.0).astype(BF16)
+        picked = dot(stacked, pick)
+        picked = picked[0:16] + picked[16:32] + picked[32:48]
+        coarse[0, at] = picked[0:8]
+        coarse[1, at] = picked[8:16]
+        return carry
+
+    lax.fori_loop(0, members, one, 0, unroll=members <= 8)
 
 
 def pcg_kernel(
     groups, members,
-    linv, pack, unpack, slots, mask, weight, load, modes, face_modes, rhs, coarse,
+    factor_hbm, load_hbm, dof_map_hbm, dof_sign_hbm, live_hbm, face_slot_hbm, face_count_hbm, coord_hbm, raw_hbm,
     out_multipliers, out_projected,
+    factor_own, load_own, dof_map_own, dof_sign_own, live_own, face_slot_own, face_count_own, coord_own, raw_own,
+    linv, pack, unpack, slots, mask, weight, modes, face_modes, rhs, coarse, load_sem,
     inverse_rows, face_in, shape_rows, gather_in, gather_out, halo_in, halo_out,
     send_gather, recv_gather, send_halo, recv_halo, send_setup, recv_setup,
 ):
+    loads = [
+        pltpu.make_async_copy(src, dst, load_sem.at[at])
+        for at, (src, dst) in enumerate((
+            (load_hbm, load_own), (dof_map_hbm, dof_map_own), (dof_sign_hbm, dof_sign_own),
+            (live_hbm, live_own), (face_slot_hbm, face_slot_own), (face_count_hbm, face_count_own),
+            (coord_hbm, coord_own), (raw_hbm, raw_own), (factor_hbm, factor_own),
+        ))
+    ]
+    for copy in loads:
+        copy.start()
+    factor, load = factor_own.at[0], load_own.at[0]
     subs, size = load.shape
     faces = pack.shape[2]
     cap = faces // 4
@@ -200,9 +234,20 @@
     )
     opposite = (RIGHT, LEFT, UP, DOWN)
 
-    def peer(step):
-        other = lax.rem(me + step, total)
-        return (other // members, lax.rem(other, members))
+    across = [lax.rem(c + step, groups) for step in range(groups)]
+    along = [lax.rem(m + step, members) for step in range(members)]
+
+    def each_peer(action):
+        if total <= 32:
+            for far in range(members - 1, -1, -1):
+                for off in range(groups - 1, -1, -1):
+                    if far or off:
+                        action((across[off], along[far]))
+        else:
+            @pl.loop(1, total)
+            def _(step):
+                other = lax.rem(me + step, total)
+                action((other // members, lax.rem(other, members)))
 
     inverse_rows[...] = jnp.zeros(inverse_rows.shape, F32)
     face_in[...] = jnp.zeros(face_in.shape, F32)
@@ -210,10 +255,16 @@
 
     barrier = pltpu.get_barrier_semaphore()
 
-    @pl.loop(1, total)
-    def _(step):
-        pl.semaphore_signal(barrier, inc=1, device_id=peer(step), device_id_type=pl.DeviceIdType.MESH)
-
+    each_peer(
+        lambda where: pl.semaphore_signal(barrier, inc=1, device_id=where, device_id_type=pl.DeviceIdType.MESH)
+    )
+    for copy in loads[:-1]:
+        copy.wait()
+    tables(
+        live_own, face_count_own.at[0], load, dof_map_own.at[0], dof_sign_own.at[0], face_slot_own.at[0],
+        coord_own.at[0], pack, unpack, slots, mask, weight, modes, face_modes, rhs,
+    )
+    coarse_layout(raw_own, coarse, groups, members)
     pl.semaphore_wait(barrier, total - 1)
 
     def remote(src, dst, send, recv, where):
@@ -259,12 +310,12 @@
         gather_out[turn] = row
         gather_in[turn, me] = row
 
-        @pl.loop(1, total)
-        def _(step):
-            remote(
+        each_peer(
+            lambda where: remote(
                 gather_out.at[turn], gather_in.at[turn, me],
-                send_gather.at[turn], recv_gather.at[turn], peer(step),
+                send_gather.at[turn], recv_gather.at[turn], where,
             ).start()
+        )
 
     def gather_view(turn):
         return gather_in.at[turn, pl.ds(0, total - 1)]
@@ -380,6 +431,8 @@
         inverse_rows[0, s] = coarse[s]
     inverse_rows[2, 0] = coarse[1]
     inverse_rows[1, 1] = coarse[0]
+    loads[-1].wait()
+    invert(factor, linv, subs)
     each_way(lambda way: face_copy(opposite[way]).wait_recv())
     each_way(lambda way: coarse_copy(opposite[way]).wait_recv())
     rights = (face_modes[1], face_in[RIGHT, 0])
@@ -444,42 +497,30 @@
     span = 16 * groups
     width = -(-span // TILE) * TILE
     message = -(-2 * span // TILE) * TILE
-    vmem = pl.BlockSpec(memory_space=pltpu.VMEM)
-    smem = pl.BlockSpec(memory_space=pltpu.SMEM)
+    args = (
+        factor, load, dof_map, dof_sign, live_count, face_slot, face_count, node_coord.transpose(0, 2, 1, 3), coarse_inverse
+    )
     shape = jax.ShapeDtypeStruct
-    prepared = pl.pallas_call(
-        setup_kernel,
-        name="setup",
-        out_shape=(
-            shape((subs, size, size), F32),
-            shape((subs, size, faces), BF16),
-            shape((subs, size, faces), BF16),
-            shape((subs, size, size), BF16),
-            shape((subs, size), F32),
-            shape((subs, size), F32),
-            shape((subs, 8, size), F32),
-            shape((subs, 8, faces), F32),
-            shape((subs, 8, TILE), F32),
-        ),
-        in_specs=[smem, smem] + [vmem] * 6,
-        out_specs=[vmem] * 9,
-        compiler_params=pltpu.CompilerParams(vmem_limit_bytes=48 * 2**20),
-    )(
-        live_count[0], face_count[0], factor[0], load[0], dof_map[0], dof_sign[0], face_slot[0], node_coord[0]
-    )
-    rows = coarse_inverse.reshape(subs, 6, groups, members, subs, 6)
-    rows = jnp.pad(rows, ((0, 0), (0, 2), (0, 0), (0, 0), (0, 0), (0, 2)))
-    rows = rows.transpose(0, 3, 1, 2, 4, 5).reshape(subs, members, 8, span)
-    rows = jnp.pad(rows, ((0, 0), (0, 0), (0, 0), (0, width - span)))
-    linv, pack, unpack, slots, mask, weight, modes, face_modes, rhs = prepared
     turns = ITERS + 2
     multipliers, projected = pl.pallas_call(
         functools.partial(pcg_kernel, groups, members),
         name="pcg",
         out_shape=(shape((subs, size), F32), shape((subs, size), F32)),
-        in_specs=[vmem] * 11,
-        out_specs=[vmem] * 2,
-        scratch_shapes=[
+        in_specs=[pl.BlockSpec(memory_space=pltpu.HBM)] * len(args),
+        out_specs=[pl.BlockSpec(memory_space=pltpu.VMEM)] * 2,
+        scratch_shapes=[pltpu.VMEM(value.shape, value.dtype) for value in args]
+        + [
+            pltpu.VMEM((subs, size, size), F32),
+            pltpu.VMEM((subs, size, faces), BF16),
+            pltpu.VMEM((subs, size, faces), BF16),
+            pltpu.VMEM((subs, size, size), BF16),
+            pltpu.VMEM((subs, size), F32),
+            pltpu.VMEM((subs, size), F32),
+            pltpu.VMEM((subs, 8, size), F32),
+            pltpu.VMEM((subs, 8, faces), F32),
+            pltpu.VMEM((subs, 8, TILE), F32),
+            pltpu.VMEM((subs, members, 8, width), F32),
+            pltpu.SemaphoreType.DMA((len(args),)),
             pltpu.VMEM((5, subs, members, 8, width), F32),
             pltpu.VMEM((4, subs, 8, faces), F32),
             pltpu.VMEM((subs, 40, size), F32),
@@ -495,9 +536,9 @@
             pltpu.SemaphoreType.DMA((2, 4)),
         ],
         compiler_params=pltpu.CompilerParams(
-            collective_id=0, has_side_effects=True, vmem_limit_bytes=48 * 2**20
+            collective_id=0, has_side_effects=True, vmem_limit_bytes=VMEM_LIMIT
         ),
-    )(linv, pack, unpack, slots, mask, weight, load[0], modes, face_modes, rhs, rows)
+    )(*args)
     return multipliers[None], projected[None]
 
 

time: 61.3 us -> 40 us (0.65)
  Pallas kernels: 51.8 us -> 36.6 us
  local copies, waits for them, and re-layouts: 8.42 us -> 2.57 us
    pallas_call x1 -> x0, Pallas kernels: 12.8 us -> none  [shards(): pl.pallas_call(setup_kernel, name='setup', out_shape=(shape((subs, size,...]
    unnamed x15 -> x2, local copies, waits for them, and re-layouts: 5.97 us -> 2.57 us
    pallas_call x1, Pallas kernels: 39 us -> 36.6 us  [shards(): pl.pallas_call(functools.partial(pcg_kernel, groups, members), name='pcg'...]
    reshape x2 -> x0, local copies, waits for them, and re-layouts: 1.98 us -> none  [the longest x1 1.32 us: shards(): rows = coarse_inverse.reshape(subs, 6, groups, members, subs, 6)]
where the time goes in v2:
time: 40 us; the launch traced here: 39.8 us
  Pallas kernels  36.6 us (92%)
  local copies, waits for them, and re-layouts  2.57 us (6%)
  between operations  0.64 us (2%)
    pallas_call x1, Pallas kernels, shards(): pl.pallas_call(functools.partial(pcg_kernel, groups, members), name='pcg'...  36.6 us
    unnamed x2, local copies, waits for them, and re-layouts  2.57 us

profile of v2, /device:TPU:0, one launch (start us, length us, event | category | flops | bytes accessed | tf_op | source)
XLA Modules:
  0.0 39.8 jit_solution(8057200590183319104)
XLA Ops:
  0.6 36.6 %pcg.1 = (f32[2,768]{1,0:T(2,128)}, f32[2,768]{1,0:T(2,128)}) custom-call(f32[1,2,768,768]{3,2,1,0:T(8,128)} %factor_hbm.1, f32[1,2,768]{2,1,0:T(2,128)} %load_hbm.1, s32[1,2,768]{2,1,0:T(2,128)} %dof_map_hbm.1, s32[1,2,768]{2,1,0:T(2,128)} %dof_sign_hbm.1, s32[1,2]{1,0:T(1,128)} %live_hbm.1, s32[1,2,4,64]{3,2,1,0:T(4,128)} %face_slot_hbm.1, ...), custom_call_target="tpu_custom_call" | custom-call | tf_op jit(solution)/shard_map/pcg/pallas_call | solution.py:505
  37.2 1.3 %copy.13 = f32[1,2,768]{2,1,0:T(2,128)} copy(f32[1,2,768]{2,1,0:T(2,128)} %bitcast.5) | data formatting | bytes 12288
  38.5 1.3 %copy.14 = f32[1,2,768]{2,1,0:T(2,128)} copy(f32[1,2,768]{2,1,0:T(2,128)} %bitcast.4) | data formatting | bytes 12288

commit v3 on v2

--- a/solution.py
+++ b/solution.py
@@ -200,11 +200,11 @@
 def pcg_kernel(
     groups, members,
     factor_hbm, load_hbm, dof_map_hbm, dof_sign_hbm, live_hbm, face_slot_hbm, face_count_hbm, coord_hbm, raw_hbm,
-    out_multipliers, out_projected,
+    out,
     factor_own, load_own, dof_map_own, dof_sign_own, live_own, face_slot_own, face_count_own, coord_own, raw_own,
     linv, pack, unpack, slots, mask, weight, modes, face_modes, rhs, coarse, load_sem,
-    inverse_rows, face_in, shape_rows, gather_in, gather_out, halo_in, halo_out,
-    send_gather, recv_gather, send_halo, recv_halo, send_setup, recv_setup,
+    inverse_rows, face_in, shape_rows, across_in, across_out, along_in, along_out, halo_in, halo_out,
+    send_across, recv_across, send_along, recv_along, send_halo, recv_halo, send_setup, recv_setup,
 ):
     loads = [
         pltpu.make_async_copy(src, dst, load_sem.at[at])
@@ -220,12 +220,10 @@
     subs, size = load.shape
     faces = pack.shape[2]
     cap = faces // 4
-    total = groups * members
     span = 16 * groups
     width = coarse.shape[-1]
-    message = gather_out.shape[-1]
+    message = across_out.shape[-1]
     c, m = lax.axis_index("group"), lax.axis_index("member")
-    me = c * members + m
     neighbours = (
         (m > 0, (c, lax.rem(m + members - 1, members))),
         (m < members - 1, (c, lax.rem(m + 1, members))),
@@ -237,17 +235,13 @@
     across = [lax.rem(c + step, groups) for step in range(groups)]
     along = [lax.rem(m + step, members) for step in range(members)]
 
-    def each_peer(action):
-        if total <= 32:
-            for far in range(members - 1, -1, -1):
-                for off in range(groups - 1, -1, -1):
-                    if far or off:
-                        action((across[off], along[far]))
-        else:
-            @pl.loop(1, total)
-            def _(step):
-                other = lax.rem(me + step, total)
-                action((other // members, lax.rem(other, members)))
+    def each_across(action):
+        for off in range(groups - 1, 0, -1):
+            action((across[off], m))
+
+    def each_along(action):
+        for far in range(members - 1, 0, -1):
+            action((c, along[far]))
 
     inverse_rows[...] = jnp.zeros(inverse_rows.shape, F32)
     face_in[...] = jnp.zeros(face_in.shape, F32)
@@ -255,9 +249,11 @@
 
     barrier = pltpu.get_barrier_semaphore()
 
-    each_peer(
-        lambda where: pl.semaphore_signal(barrier, inc=1, device_id=where, device_id_type=pl.DeviceIdType.MESH)
-    )
+    def greet(where):
+        pl.semaphore_signal(barrier, inc=1, device_id=where, device_id_type=pl.DeviceIdType.MESH)
+
+    each_across(greet)
+    each_along(greet)
     for copy in loads[:-1]:
         copy.wait()
     tables(
@@ -265,7 +261,7 @@
         coord_own.at[0], pack, unpack, slots, mask, weight, modes, face_modes, rhs,
     )
     coarse_layout(raw_own, coarse, groups, members)
-    pl.semaphore_wait(barrier, total - 1)
+    pl.semaphore_wait(barrier, groups + members - 2)
 
     def remote(src, dst, send, recv, where):
         return pltpu.make_async_remote_copy(
@@ -306,23 +302,37 @@
             def _():
                 action(way)
 
+    def across_view(turn):
+        return across_in.at[turn, pl.ds(0, groups - 1)]
+
+    def along_view(turn):
+        return along_in.at[turn, pl.ds(0, members - 1)]
+
+    def wait_all(view, sem):
+        pltpu.make_async_copy(view, view, sem).wait()
+
     def gather_start(turn, row):
-        gather_out[turn] = row
-        gather_in[turn, me] = row
-
-        each_peer(
+        across_out[turn] = row
+        across_in[turn, c] = row
+        each_across(
             lambda where: remote(
-                gather_out.at[turn], gather_in.at[turn, me],
-                send_gather.at[turn], recv_gather.at[turn], where,
+                across_out.at[turn], across_in.at[turn, c], send_across.at[turn], recv_across.at[turn], where
             ).start()
         )
 
-    def gather_view(turn):
-        return gather_in.at[turn, pl.ds(0, total - 1)]
+    def gather_middle(turn):
+        wait_all(across_view(turn), recv_across.at[turn])
+        row = jnp.sum(across_in[turn], axis=0)
+        along_out[turn] = row
+        along_in[turn, m] = row
+        each_along(
+            lambda where: remote(
+                along_out.at[turn], along_in.at[turn, m], send_along.at[turn], recv_along.at[turn], where
+            ).start()
+        )
 
     def gather_wait(turn):
-        view = gather_view(turn)
-        pltpu.make_async_copy(view, view, recv_gather.at[turn]).wait()
+        wait_all(along_view(turn), recv_along.at[turn])
 
     lane_row = iota((1, message), 1)
 
@@ -340,7 +350,7 @@
     places = [placing(s) for s in range(subs)]
 
     def coarse_sum(turn):
-        summed = jnp.sum(gather_in[turn].reshape(groups, members, 1, message), axis=0).reshape(members, message)
+        summed = along_in[turn].reshape(members, message)
         if span >= TILE:
             low, high = summed[:, :span], summed[:, span : 2 * span]
         else:
@@ -402,6 +412,7 @@
         for at, value in enumerate(scalars):
             row = row + jnp.where(lane_row == 16 * c + spare[at], value, 0.0)
         gather_start(turn, row)
+        gather_middle(turn)
         each_way(lambda way: halo_copy(turn - 1, opposite[way]).wait_recv())
         arrived = halo_in.at[turn - 1]
         rights = (outgoing[1], arrived[RIGHT, 0])
@@ -432,6 +443,7 @@
     inverse_rows[2, 0] = coarse[1]
     inverse_rows[1, 1] = coarse[0]
     loads[-1].wait()
+    gather_middle(0)
     invert(factor, linv, subs)
     each_way(lambda way: face_copy(opposite[way]).wait_recv())
     each_way(lambda way: coarse_copy(opposite[way]).wait_recv())
@@ -476,16 +488,16 @@
         projected = [projected[s] - step * direction_change[s] for s in range(subs)]
     for s in range(subs):
         ordered = row_times([multipliers[s], projected[s]], slots[s])
-        out_multipliers[s : s + 1, :] = ordered[0]
-        out_projected[s : s + 1, :] = ordered[1]
+        out[0, s : s + 1, :] = ordered[0]
+        out[1, s : s + 1, :] = ordered[1]
 
     each_way(lambda way: face_copy(way).wait_send())
     each_way(lambda way: coarse_copy(way).wait_send())
     for turn in range(ITERS + 1):
         each_way(lambda way: halo_copy(turn, way).wait_send())
     for turn in range(ITERS + 2):
-        view = gather_view(turn)
-        pltpu.make_async_copy(view, view, send_gather.at[turn]).wait()
+        wait_all(across_view(turn), send_across.at[turn])
+        wait_all(along_view(turn), send_along.at[turn])
 
 
 def shards(
@@ -502,12 +514,12 @@
     )
     shape = jax.ShapeDtypeStruct
     turns = ITERS + 2
-    multipliers, projected = pl.pallas_call(
+    result = pl.pallas_call(
         functools.partial(pcg_kernel, groups, members),
         name="pcg",
-        out_shape=(shape((subs, size), F32), shape((subs, size), F32)),
+        out_shape=shape((2, subs, size), F32),
         in_specs=[pl.BlockSpec(memory_space=pltpu.HBM)] * len(args),
-        out_specs=[pl.BlockSpec(memory_space=pltpu.VMEM)] * 2,
+        out_specs=pl.BlockSpec(memory_space=pltpu.VMEM),
         scratch_shapes=[pltpu.VMEM(value.shape, value.dtype) for value in args]
         + [
             pltpu.VMEM((subs, size, size), F32),
@@ -524,10 +536,14 @@
             pltpu.VMEM((5, subs, members, 8, width), F32),
             pltpu.VMEM((4, subs, 8, faces), F32),
             pltpu.VMEM((subs, 40, size), F32),
-            pltpu.VMEM((turns, groups * members, 1, message), F32),
+            pltpu.VMEM((turns, groups, 1, message), F32),
+            pltpu.VMEM((turns, 1, message), F32),
+            pltpu.VMEM((turns, members, 1, message), F32),
             pltpu.VMEM((turns, 1, message), F32),
             pltpu.VMEM((turns - 1, 4, subs, 1, faces), F32),
             pltpu.VMEM((turns - 1, subs, 1, faces), F32),
+            pltpu.SemaphoreType.DMA((turns,)),
+            pltpu.SemaphoreType.DMA((turns,)),
             pltpu.SemaphoreType.DMA((turns,)),
             pltpu.SemaphoreType.DMA((turns,)),
             pltpu.SemaphoreType.DMA((turns - 1, 4)),
@@ -539,7 +555,7 @@
             collective_id=0, has_side_effects=True, vmem_limit_bytes=VMEM_LIMIT
         ),
     )(*args)
-    return multipliers[None], projected[None]
+    return result[0:1], result[1:2]
 
 
 def solution(mesh):

time: 40 us -> 51.7 us (1.29)
  Pallas kernels: 36.6 us -> 49.5 us
  local copies, waits for them, and re-layouts: 2.57 us -> 1.31 us
    pallas_call x1, Pallas kernels: 36.6 us -> 49.5 us  [shards(): pl.pallas_call(functools.partial(pcg_kernel, groups, members), name='pcg'...]
    unnamed x2 -> x0, local copies, waits for them, and re-layouts: 2.57 us -> none
    slice x0 -> x1, local copies, waits for them, and re-layouts: none -> 1.31 us  [shards(): return (result[0:1], result[1:2])]
where the time goes in v3:
time: 51.7 us; the launch traced here: 51.4 us
  Pallas kernels  49.5 us (96%)
  local copies, waits for them, and re-layouts  1.31 us (3%)
  between operations  0.64 us (1%)
    pallas_call x1, Pallas kernels, shards(): pl.pallas_call(functools.partial(pcg_kernel, groups, members), name='pcg'...  49.5 us
    slice x1, local copies, waits for them, and re-layouts, shards(): return (result[0:1], result[1:2])  1.31 us

profile of v3, /device:TPU:0, one launch (start us, length us, event | category | flops | bytes accessed | tf_op | source)
XLA Modules:
  0.0 51.4 jit_solution(14009833322540505322)
XLA Ops:
  0.6 49.5 %pcg.1 = f32[2,2,768]{2,1,0:T(2,128)} custom-call(f32[1,2,768,768]{3,2,1,0:T(8,128)} %factor_hbm.1, f32[1,2,768]{2,1,0:T(2,128)} %load_hbm.1, s32[1,2,768]{2,1,0:T(2,128)} %dof_map_hbm.1, s32[1,2,768]{2,1,0:T(2,128)} %dof_sign_hbm.1, s32[1,2]{1,0:T(1,128)} %live_hbm.1, s32[1,2,4,64]{3,2,1,0:T(4,128)} %face_slot_hbm.1, s32[1,2,4]{2,1,0:T(2,128)} %face_count_hbm.1, ...), custom_call_target="tpu_custom_call" | custom-call | tf_op jit(solution)/shard_map/pcg/pallas_call | solution.py:517
  50.1 1.3 %fusion = (f32[1,2,768]{2,1,0:T(2,128)}, f32[1,2,768]{2,1,0:T(2,128)}) fusion(f32[2,2,768]{2,1,0:T(2,128)} %pcg.1), kind=kLoop, calls=%fused_computation | loop fusion | bytes 24576 | tf_op jit(solution)/shard_map/slice | solution.py:558

commit v4 on v2

--- a/solution.py
+++ b/solution.py
@@ -39,6 +39,11 @@
 def mm(left, right):
     left_hi, left_lo = parts_of(left, 2)
     right_hi, right_lo = parts_of(right, 2)
+    if left.shape[1] == TILE:
+        deep = dot(
+            jnp.concatenate([left_hi, left_lo], axis=1), jnp.concatenate([right_hi, right_hi], axis=0)
+        )
+        return deep + dot(left_hi, right_lo)
     return dot(left_hi, right_hi) + (dot(left_hi, right_lo) + dot(left_lo, right_hi))
 
 
@@ -78,7 +83,10 @@
     source, target = iota(wide, 0), iota(wide, 1)
     spread = (((source & (BASE - 1)) == (target >> 7)) & ((source >> shift) == ((target & 127) >> shift)))
     spread = jnp.where(spread, 1.0, 0.0).astype(BF16)
-    columns = sum(dot(part, spread) for part in parts_of(packed, 3))
+    high, middle, low = parts_of(packed, 3)
+    columns = dot(
+        jnp.concatenate([high, middle], axis=1), jnp.concatenate([spread, spread], axis=0)
+    ) + dot(low, spread)
     within = iota((count, BASE, TILE), 1)
     solved = jnp.where(within == (iota((count, BASE, TILE), 2) & (BASE - 1)), 1.0, 0.0)
     for m in range(BASE):
@@ -137,11 +145,11 @@
                 limit = jnp.where(lane // cap == at, at * cap + face_count[s : s + 1, f : f + 1], limit)
             face_row = jnp.where(lane < limit, face_row, -1)
             hit = jnp.where(iota((size, 4 * cap), 0) == face_row, 1.0, 0.0).astype(BF16)
-            return dot(slot_rows, hit).astype(BF16)
-
-        outgoing = table_of((0, 1, 2, 3))
+            return dot(slot_rows, hit)
+
+        outgoing = table_of((0, 1, 2, 3)).astype(BF16)
         pack[s] = outgoing
-        unpack[s] = table_of((1, 0, 3, 2))
+        unpack[s] = table_of((1, 0, 3, 2)).T.astype(BF16)
         live_row = jnp.abs(dot(jnp.ones((8, size), BF16), slot_rows, NT))[0:1]
         shared = dot(jnp.ones((8, 4 * cap), BF16), jnp.abs(outgoing), NT)[0:1]
         mask[s : s + 1, :] = live_row
@@ -200,7 +208,7 @@
 def pcg_kernel(
     groups, members,
     factor_hbm, load_hbm, dof_map_hbm, dof_sign_hbm, live_hbm, face_slot_hbm, face_count_hbm, coord_hbm, raw_hbm,
-    out_multipliers, out_projected,
+    out,
     factor_own, load_own, dof_map_own, dof_sign_own, live_own, face_slot_own, face_count_own, coord_own, raw_own,
     linv, pack, unpack, slots, mask, weight, modes, face_modes, rhs, coarse, load_sem,
     inverse_rows, face_in, shape_rows, gather_in, gather_out, halo_in, halo_out,
@@ -390,10 +398,6 @@
         )
 
     def project(turn, fields, scalars):
-        outgoing = [row_times([fields[s]], pack[s])[0] for s in range(subs)]
-        for s in range(subs):
-            halo_out[turn - 1, s] = outgoing[s]
-        each_way(lambda way: halo_copy(turn - 1, way).start())
         row = jnp.zeros((1, message), F32)
         for s in range(subs):
             column = jnp.sum(shape_rows[s] * fields[s], axis=1, keepdims=True)
@@ -402,6 +406,10 @@
         for at, value in enumerate(scalars):
             row = row + jnp.where(lane_row == 16 * c + spare[at], value, 0.0)
         gather_start(turn, row)
+        outgoing = [row_times([fields[s]], pack[s])[0] for s in range(subs)]
+        for s in range(subs):
+            halo_out[turn - 1, s] = outgoing[s]
+        each_way(lambda way: halo_copy(turn - 1, way).start())
         each_way(lambda way: halo_copy(turn - 1, opposite[way]).wait_recv())
         arrived = halo_in.at[turn - 1]
         rights = (outgoing[1], arrived[RIGHT, 0])
@@ -409,7 +417,7 @@
         assembled = []
         for s in range(subs):
             incoming = from_faces(rights[s], lefts[s], arrived[UP, s], arrived[DOWN, s])
-            assembled.append(fields[s] + row_times([incoming], unpack[s], NT)[0])
+            assembled.append(fields[s] + row_times([incoming], unpack[s])[0])
         gather_wait(turn)
         values = coarse_sum(turn)
         fixes = correction(values)
@@ -444,7 +452,7 @@
             [jnp.where(block == (1, 0, 3, 2)[f], sources[f], 0.0) for f in range(4)], axis=0
         ).astype(BF16)
         shape_rows[s, 0:8, :] = modes[s]
-        shape_rows[s, 8:40, :] = dot(spread, unpack[s], NT)
+        shape_rows[s, 8:40, :] = dot(spread, unpack[s])
     gather_wait(0)
     multipliers = correction(coarse_sum(0))
     start = apply_dual([load[s : s + 1, :] - multipliers[s] for s in range(subs)])
@@ -476,8 +484,8 @@
         projected = [projected[s] - step * direction_change[s] for s in range(subs)]
     for s in range(subs):
         ordered = row_times([multipliers[s], projected[s]], slots[s])
-        out_multipliers[s : s + 1, :] = ordered[0]
-        out_projected[s : s + 1, :] = ordered[1]
+        out[0, s : s + 1, :] = ordered[0]
+        out[1, s : s + 1, :] = ordered[1]
 
     each_way(lambda way: face_copy(way).wait_send())
     each_way(lambda way: coarse_copy(way).wait_send())
@@ -502,17 +510,17 @@
     )
     shape = jax.ShapeDtypeStruct
     turns = ITERS + 2
-    multipliers, projected = pl.pallas_call(
+    result = pl.pallas_call(
         functools.partial(pcg_kernel, groups, members),
         name="pcg",
-        out_shape=(shape((subs, size), F32), shape((subs, size), F32)),
+        out_shape=shape((2, subs, size), F32),
         in_specs=[pl.BlockSpec(memory_space=pltpu.HBM)] * len(args),
-        out_specs=[pl.BlockSpec(memory_space=pltpu.VMEM)] * 2,
+        out_specs=pl.BlockSpec(memory_space=pltpu.VMEM),
         scratch_shapes=[pltpu.VMEM(value.shape, value.dtype) for value in args]
         + [
             pltpu.VMEM((subs, size, size), F32),
             pltpu.VMEM((subs, size, faces), BF16),
-            pltpu.VMEM((subs, size, faces), BF16),
+            pltpu.VMEM((subs, faces, size), BF16),
             pltpu.VMEM((subs, size, size), BF16),
             pltpu.VMEM((subs, size), F32),
             pltpu.VMEM((subs, size), F32),
@@ -539,7 +547,7 @@
             collective_id=0, has_side_effects=True, vmem_limit_bytes=VMEM_LIMIT
         ),
     )(*args)
-    return multipliers[None], projected[None]
+    return result[0:1], result[1:2]
 
 
 def solution(mesh):

time: 40 us -> 37.9 us (0.948)
  local copies, waits for them, and re-layouts: 2.57 us -> 1.31 us
  Pallas kernels: 36.6 us -> 35.7 us
    unnamed x2 -> x0, local copies, waits for them, and re-layouts: 2.57 us -> none
    slice x0 -> x1, local copies, waits for them, and re-layouts: none -> 1.31 us  [shards(): return (result[0:1], result[1:2])]
    pallas_call x1, Pallas kernels: 36.6 us -> 35.7 us  [shards(): pl.pallas_call(functools.partial(pcg_kernel, groups, members), name='pcg'...]
where the time goes in v4:
time: 37.9 us; the launch traced here: 37.7 us
  Pallas kernels  35.7 us (94%)
  local copies, waits for them, and re-layouts  1.31 us (3%)
  between operations  0.64 us (2%)
    pallas_call x1, Pallas kernels, shards(): pl.pallas_call(functools.partial(pcg_kernel, groups, members), name='pcg'...  35.7 us
    slice x1, local copies, waits for them, and re-layouts, shards(): return (result[0:1], result[1:2])  1.31 us

profile of v4, /device:TPU:0, one launch (start us, length us, event | category | flops | bytes accessed | tf_op | source)
XLA Modules:
  0.0 37.7 jit_solution(4323429972378108609)
XLA Ops:
  0.6 35.7 %pcg.1 = f32[2,2,768]{2,1,0:T(2,128)} custom-call(f32[1,2,768,768]{3,2,1,0:T(8,128)} %factor_hbm.1, f32[1,2,768]{2,1,0:T(2,128)} %load_hbm.1, s32[1,2,768]{2,1,0:T(2,128)} %dof_map_hbm.1, s32[1,2,768]{2,1,0:T(2,128)} %dof_sign_hbm.1, s32[1,2]{1,0:T(1,128)} %live_hbm.1, s32[1,2,4,64]{3,2,1,0:T(4,128)} %face_slot_hbm.1, s32[1,2,4]{2,1,0:T(2,128)} %face_count_hbm.1, ...), custom_call_target="tpu_custom_call" | custom-call | tf_op jit(solution)/shard_map/pcg/pallas_call | solution.py:513
  36.4 1.3 %fusion = (f32[1,2,768]{2,1,0:T(2,128)}, f32[1,2,768]{2,1,0:T(2,128)}) fusion(f32[2,2,768]{2,1,0:T(2,128)} %pcg.1), kind=kLoop, calls=%fused_computation | loop fusion | bytes 24576 | tf_op jit(solution)/shard_map/slice | solution.py:550

commit v5 on v4

--- a/solution.py
+++ b/solution.py
@@ -15,7 +15,6 @@
 LEFT, RIGHT, DOWN, UP = range(4)
 F32 = jnp.float32
 BF16 = jnp.bfloat16
-NT = (((1,), (1,)), ((), ()))
 NN = (((1,), (0,)), ((), ()))
 
 
@@ -137,21 +136,25 @@
         slot_rows = jnp.where(iota((size, size), 0) == dof_map[s : s + 1, :], sign_row, 0.0).astype(BF16)
         slots[s] = slot_rows
 
-        def table_of(order):
+        def hits(order):
             face_row = jnp.concatenate([face_slot[s, f : f + 1, :] for f in order], axis=1)
             lane = iota((1, 4 * cap), 1)
             limit = jnp.zeros((1, 4 * cap), jnp.int32)
             for at, f in enumerate(order):
                 limit = jnp.where(lane // cap == at, at * cap + face_count[s : s + 1, f : f + 1], limit)
             face_row = jnp.where(lane < limit, face_row, -1)
-            hit = jnp.where(iota((size, 4 * cap), 0) == face_row, 1.0, 0.0).astype(BF16)
-            return dot(slot_rows, hit)
-
-        outgoing = table_of((0, 1, 2, 3)).astype(BF16)
+            return jnp.where(iota((size, 4 * cap), 0) == face_row, 1.0, 0.0).astype(BF16)
+
+        sign_column = jnp.broadcast_to(sign_row, (TILE, size)).T.astype(BF16)
+        product = dot(
+            slot_rows, jnp.concatenate([hits((0, 1, 2, 3)), hits((1, 0, 3, 2)), sign_column], axis=1)
+        )
+        outgoing = product[:, : 4 * cap].astype(BF16)
         pack[s] = outgoing
-        unpack[s] = table_of((1, 0, 3, 2)).T.astype(BF16)
-        live_row = jnp.abs(dot(jnp.ones((8, size), BF16), slot_rows, NT))[0:1]
-        shared = dot(jnp.ones((8, 4 * cap), BF16), jnp.abs(outgoing), NT)[0:1]
+        turned = product[:, 4 * cap :].T
+        unpack[s] = turned[: 4 * cap].astype(BF16)
+        live_row = turned[4 * cap : 4 * cap + 1]
+        shared = jnp.sum(jnp.abs(turned[: 4 * cap]), axis=0, keepdims=True)
         mask[s : s + 1, :] = live_row
         weight[s : s + 1, :] = live_row * (1.0 - 0.5 * shared)
         position = jnp.concatenate([coord[axis, s : s + 1, :] for axis in range(3)], axis=0)

time: 37.9 us -> 37.6 us (level)
  no operation moved by 1% of the time
where the time goes in v5:
time: 37.6 us; the launch traced here: 37.3 us
  Pallas kernels  35.4 us (94%)
  local copies, waits for them, and re-layouts  1.31 us (3%)
  between operations  0.64 us (2%)
    pallas_call x1, Pallas kernels, shards(): pl.pallas_call(functools.partial(pcg_kernel, groups, members), name='pcg'...  35.4 us
    slice x1, local copies, waits for them, and re-layouts, shards(): return (result[0:1], result[1:2])  1.31 us

profile of v5, /device:TPU:0, one launch (start us, length us, event | category | flops | bytes accessed | tf_op | source)
XLA Modules:
  0.0 37.3 jit_solution(4783374157438435202)
XLA Ops:
  0.6 35.4 %pcg.1 = f32[2,2,768]{2,1,0:T(2,128)} custom-call(f32[1,2,768,768]{3,2,1,0:T(8,128)} %factor_hbm.1, f32[1,2,768]{2,1,0:T(2,128)} %load_hbm.1, s32[1,2,768]{2,1,0:T(2,128)} %dof_map_hbm.1, s32[1,2,768]{2,1,0:T(2,128)} %dof_sign_hbm.1, s32[1,2]{1,0:T(1,128)} %live_hbm.1, s32[1,2,4,64]{3,2,1,0:T(4,128)} %face_slot_hbm.1, s32[1,2,4]{2,1,0:T(2,128)} %face_count_hbm.1, ...), custom_call_target="tpu_custom_call" | custom-call | tf_op jit(solution)/shard_map/pcg/pallas_call | solution.py:516
  36.0 1.3 %fusion = (f32[1,2,768]{2,1,0:T(2,128)}, f32[1,2,768]{2,1,0:T(2,128)}) fusion(f32[2,2,768]{2,1,0:T(2,128)} %pcg.1), kind=kLoop, calls=%fused_computation | loop fusion | bytes 24576 | tf_op jit(solution)/shard_map/slice | solution.py:553
